TPU v7x, 128 devices: a whole 4x4x4 slice. The times are simulated.
128 devices in a mesh: dp: 128 (over x, z, y, core).
Axes of the slice: x: 4, y: 4, z: 4, core: 2. Of those that a mesh axis runs over, the one named last changes fastest.
Arguments:
- grad: float32 [4096, 8192], P('dp'), may hold values from -8 to 8
- block_owner: int32 [128], replicated, may hold values from 0 to 127, as said below
- left_factor: float32 [256, 512, 512], P('dp'), may hold values from -3 to 3
- right_factor: float32 [256, 512, 512], P('dp'), may hold values from -3 to 3
- left_basis: float32 [256, 512, 512], P('dp'), may hold values from -0.25 to 0.25
- right_basis: float32 [256, 512, 512], P('dp'), may hold values from -0.25 to 0.25
- first_moment: float32 [256, 512, 512], P('dp'), may hold values from -0.072 to 0.072
- second_moment: float32 [256, 512, 512], P('dp'), may hold values from 0.0002 to 0.002
Outputs:
- updates: bfloat16 [4096, 8192], P('dp')
- new_left: float32 [256, 512, 512], P('dp')
- new_right: float32 [256, 512, 512], P('dp')
- new_first: float32 [256, 512, 512], P('dp')
- new_second: float32 [256, 512, 512], P('dp')
Inputs may be any that keep to these rules, and one draw needn't show every extreme that they name: `block_owner`: block b covers rows 512 * (b // 16) to 512 * (b // 16) + 511 of the stacked matrices. The 16 blocks of one row of blocks have different owners. A quarter of the devices own 2 blocks each, half own one block and the rest own none.
All inputs are finite; a program needn't handle non-finite values.
Results may differ from a plain program's by a relative error of at most 0.001.
Values may be sent and summed in bfloat16 or wider, within the bound.
A program may use at most 128 MiB of HBM per device.

v0:
```python
import jax
import jax.numpy as jnp
from jax import lax
from jax.sharding import PartitionSpec as P

full_precision = lax.Precision.HIGHEST
first_correction = 1.0 - 0.9**10
second_correction = 1.0 - 0.95**10


def matmul_full(left_arr, right_arr):
    return jnp.dot(left_arr, right_arr, precision=full_precision)


def block_slots(block_owner):
    count = block_owner.shape[0]
    positions = jnp.arange(count, dtype=jnp.int32)
    same_owner = block_owner[:, None] == block_owner[None, :]
    earlier = positions[None, :] < positions[:, None]
    return jnp.sum(jnp.where(same_owner & earlier, 1, 0), axis=1).astype(jnp.int32)


def soap_block(grad_block, left_stat, right_stat, left_rot, right_rot, first_stat, second_stat):
    next_left = 0.95 * left_stat + 0.05 * matmul_full(grad_block, grad_block.T)
    next_right = 0.95 * right_stat + 0.05 * matmul_full(grad_block.T, grad_block)
    rotated = matmul_full(matmul_full(left_rot.T, grad_block), right_rot)
    next_first = 0.9 * first_stat + 0.1 * rotated
    next_second = 0.95 * second_stat + 0.05 * rotated * rotated
    direction = next_first / first_correction / (jnp.sqrt(next_second / second_correction) + 1e-08)
    update = matmul_full(matmul_full(left_rot, direction), right_rot.T).astype(jnp.bfloat16)
    return (next_left, next_right, next_first, next_second, update)


def clip_scale(squares, entries):
    summed = lax.psum(squares, "dp")
    return jnp.minimum(1.0, 0.04 / (jnp.sqrt(summed / entries) + 1e-06))


def per_device(
    grad,
    block_owner,
    left_factor,
    right_factor,
    left_basis,
    right_basis,
    first_moment,
    second_moment,
):
    devices = lax.axis_size("dp")
    my_index = lax.axis_index("dp")
    dev_rows, row_width = grad.shape
    block_order = left_factor.shape[1]
    capacity = left_factor.shape[0]
    columns = row_width // block_order
    group_size = block_order // dev_rows
    my_group = my_index // group_size
    entries = dev_rows * row_width * devices
    slot_of = block_slots(block_owner)
    block_ids = jnp.arange(block_owner.shape[0], dtype=jnp.int32)
    owned_block = []
    present = []
    for slot_index in range(capacity):
        matched = (block_owner == my_index) & (slot_of == slot_index)
        owned_block.append(jnp.sum(jnp.where(matched, block_ids, 0)))
        present.append(jnp.any(matched))
    squares = jnp.sum(grad * grad)
    outgoing = grad * clip_scale(squares, entries)
    row_owner = lax.dynamic_slice_in_dim(block_owner, my_group * columns, columns)
    pieces = outgoing.reshape(dev_rows, columns, block_order).transpose(1, 0, 2)
    sendbuf = jnp.zeros((devices, dev_rows, block_order), jnp.float32).at[row_owner].set(pieces)
    arrived = lax.all_to_all(sendbuf, "dp", split_axis=0, concat_axis=0, tiled=True)
    gathered = []
    for slot_index in range(capacity):
        first_row = owned_block[slot_index] // columns * group_size
        rows_in = lax.dynamic_slice_in_dim(arrived, first_row, group_size, 0)
        gathered.append(rows_in.reshape(block_order, block_order))
    results = []
    for slot_index in range(capacity):
        results.append(
            soap_block(
                gathered[slot_index],
                left_factor[slot_index],
                right_factor[slot_index],
                left_basis[slot_index],
                right_basis[slot_index],
                first_moment[slot_index],
                second_moment[slot_index],
            )
        )
    old_states = (left_factor, right_factor, first_moment, second_moment)
    new_states = []
    for state_pos in range(4):
        new_states.append(
            jnp.stack(
                [
                    jnp.where(
                        present[slot_index],
                        results[slot_index][state_pos],
                        old_states[state_pos][slot_index],
                    )
                    for slot_index in range(capacity)
                ]
            )
        )
    backbuf = jnp.zeros((devices, dev_rows, block_order), jnp.bfloat16)
    for slot_index in range(capacity):
        first_row = owned_block[slot_index] // columns * group_size
        current = lax.dynamic_slice_in_dim(backbuf, first_row, group_size, 0)
        fresh_rows = jnp.where(
            present[slot_index],
            results[slot_index][4].reshape(group_size, dev_rows, block_order),
            current,
        )
        backbuf = lax.dynamic_update_slice_in_dim(backbuf, fresh_rows, first_row, 0)
    returned = lax.all_to_all(backbuf, "dp", split_axis=0, concat_axis=0, tiled=True)
    updates = returned[row_owner].transpose(1, 0, 2).reshape(dev_rows, row_width)
    return (updates, new_states[0], new_states[1], new_states[2], new_states[3])


def solution(mesh):
    in_specs = (
        P("dp", None),
        P(),
        P("dp", None, None),
        P("dp", None, None),
        P("dp", None, None),
        P("dp", None, None),
        P("dp", None, None),
        P("dp", None, None),
    )
    out_specs = (
        P("dp", None),
        P("dp", None, None),
        P("dp", None, None),
        P("dp", None, None),
        P("dp", None, None),
    )
    return jax.shard_map(
        per_device, mesh=mesh, in_specs=in_specs, out_specs=out_specs, check_vma=False
    )
```

profile of v0, /device:TPU:0, one launch (start us, length us, event | category | flops | bytes accessed | tf_op | source)
XLA Modules:
  0.0 289.3 jit_solution(16917544083470563503)
XLA Ops:
  0.6 2.1 multiply_reduce_fusion
  2.8 68.2 %psum.7 = f32[]{:T(128)} all-reduce(f32[]{:T(128)} %multiply_reduce_fusion), channel_id=1, replica_groups=mesh['dp'=128] {'dp'}, use_global_device_ids=true, to_apply=%region_3.4 | all-reduce | flops 1 | bytes 8 | tf_op jit(solution)/shard_map/psum | solution.py:35
  73.2 4.3 %broadcast_in_dim.28 = f32[128,32,512]{2,1,0:T(8,128)} broadcast(f32[]{:T(128)} %constant.66.clone.1), dimensions={} | broadcast | bytes 8388612 | tf_op jit(solution)/shard_map/broadcast_in_dim | solution.py:70
  77.5 3.0 %scatter_fusion = f32[128,32,512]{2,1,0:T(8,128)} fusion(f32[128,32,512]{2,1,0:T(8,128)} %broadcast_in_dim.28, s32[16]{0:T(128)S(1)} %compare_select_fusion, f32[16,32,512]{2,1,0:T(8,128)S(1)} %bitcast.157), kind=kCustom, calls=%fused_computation.1 | custom fusion | bytes 3145792 | tf_op jit(solution)/shard_map/scatter | solution.py:70
  80.4 6.4 %all-to-all-start = ((f32[128,32,512]{2,1,0:T(8,128)}), f32[128,32,512]{2,1,0:T(8,128)}, u32[]{:S(2)}, u32[]{:S(2)}) async-start(f32[128,32,512]{2,1,0:T(8,128)} %scatter_fusion), calls=%async_computation | async-start | bytes 16777216 | tf_op jit(solution)/shard_map/all_to_all | solution.py:71
  93.5 99.0 %all-to-all-done = f32[128,32,512]{2,1,0:T(8,128)} async-done(((f32[128,32,512]{2,1,0:T(8,128)}), f32[128,32,512]{2,1,0:T(8,128)}, u32[]{:S(2)}, u32[]{:S(2)}) %all-to-all-start) | async-done | bytes 8388640 | tf_op jit(solution)/shard_map/all_to_all | solution.py:71
  192.5 1.9 constant_dynamic-slice_fusion
  196.6 1.9 fusion.33
  198.5 1.9 fusion.19
  200.4 1.9 fusion.29
  202.3 4.1 %fusion.31 = f32[512,512]{1,0:T(8,128)S(1)} fusion(f32[2,512,512]{2,1,0:T(8,128)S(1)} %copy-done.2, f32[512,512]{1,0:T(8,128)S(1)} %fusion.29, f32[2,512,512]{2,1,0:T(8,128)S(1)} %copy-done.4, f32[2,512,512]{2,1,0:T(8,128)S(1)} %copy-done.5), kind=kOutput, calls=%fused_computation.56 | convolution fusion | flops 1613496320 | bytes 5242880 | tf_op jit(solution)/shard_map/dot_general | solution.py:12
  206.4 4.3 %fusion.21 = f32[512,512]{1,0:T(8,128)S(1)} fusion(f32[2,512,512]{2,1,0:T(8,128)S(1)} %copy-done.2, f32[512,512]{1,0:T(8,128)S(1)} %fusion.19, f32[2,512,512]{2,1,0:T(8,128)S(1)} %copy-done.4, f32[2,512,512]{2,1,0:T(8,128)S(1)} %copy-done.5), kind=kOutput, calls=%fused_computation.42 | convolution fusion | flops 1613496320 | bytes 5242880 | tf_op jit(solution)/shard_map/dot_general | solution.py:12
  210.7 3.5 %convolution_convert_fusion = bf16[512,512]{1,0:T(8,128)(2,1)S(1)} fusion(f32[512,512]{1,0:T(8,128)S(1)} %fusion.21, f32[2,512,512]{2,1,0:T(8,128)S(1)} %copy-done), kind=kOutput, calls=%fused_computation.26 | convolution fusion | flops 1610874880 | bytes 2621440 | tf_op jit(solution)/shard_map/dot_general | solution.py:12
  214.2 4.1 %fusion.14 = bf16[512,512]{1,0:T(8,128)(2,1)S(1)} fusion(f32[512,512]{1,0:T(8,128)S(1)} %fusion.31, f32[2,512,512]{2,1,0:T(8,128)S(1)} %copy-done, pred[]{:T(512)} %get-tuple-element.17), kind=kOutput, calls=%fused_computation.28 | convolution fusion | flops 1611137024 | bytes 2621441 | tf_op jit(solution)/shard_map/dot_general | solution.py:12
  218.4 2.5 broadcast_in_dim.25
  221.7 2.6 select_dynamic-update-slice_fusion
  224.3 8.5 %all-to-all-start.1 = ((bf16[128,32,512]{2,1,0:T(8,128)(2,1)}), bf16[128,32,512]{2,1,0:T(8,128)(2,1)}, u32[]{:S(2)}, u32[]{:S(2)}) async-start(bf16[128,32,512]{2,1,0:T(8,128)(2,1)} %select_dynamic-update-slice_fusion), calls=%async_computation.1 | async-start | bytes 8388608 | tf_op jit(solution)/shard_map/all_to_all | solution.py:115
  232.9 4.6 %fusion.36 = (f32[1,512,512]{2,1,0:T(8,128)S(1)}, f32[1,512,512]{2,1,0:T(8,128)S(1)}, f32[1,512,512]{2,1,0:T(8,128)S(1)}, f32[1,512,512]{2,1,0:T(8,128)S(1)}) fusion(f32[2,512,512]{2,1,0:T(8,128)} %param.14, pred[]{:T(512)} %get-tuple-element.17, f32[512,512]{1,0:T(8,128)} %copy-done.1, f32[512,512]{1,0:T(8,128)S(1)} %fusion.19, pred[]{:T(512)} %get-tuple-element.5, ...), kind=kLoop, calls=%fused_computation.63 | loop fusion | flops 4718592 | bytes 10485762 | tf_op jit(solution)/shard_map/stack | solution.py:94
  241.3 2.6 fusion.10
  243.9 2.6 fusion.13
  248.8 2.6 fusion.5
  251.4 2.6 fusion.7
  255.4 30.1 %all-to-all-done.1 = bf16[128,32,512]{2,1,0:T(8,128)(2,1)} async-done(((bf16[128,32,512]{2,1,0:T(8,128)(2,1)}), bf16[128,32,512]{2,1,0:T(8,128)(2,1)}, u32[]{:S(2)}, u32[]{:S(2)}) %all-to-all-start.1) | async-done | bytes 4194336 | tf_op jit(solution)/shard_map/all_to_all | solution.py:115
  285.5 2.8 gather_fusion
  (30 shorter events, 14.5 us)
Async XLA Ops:
  71.7 1.4 copy-start.6
  80.4 112.1 %all-to-all-start = ((f32[128,32,512]{2,1,0:T(8,128)}), f32[128,32,512]{2,1,0:T(8,128)}, u32[]{:S(2)}, u32[]{:S(2)}) async-start(f32[128,32,512]{2,1,0:T(8,128)} %scatter_fusion), calls=%async_computation | async-start | bytes 16777216 | tf_op jit(solution)/shard_map/all_to_all | solution.py:71
  192.5 2.2 copy-start.2
  196.6 1.9 copy-start
  198.5 3.8 %copy-start.5 = (f32[2,512,512]{2,1,0:T(8,128)S(1)}, f32[2,512,512]{2,1,0:T(8,128)}, u32[]{:S(2)}) copy-start(f32[2,512,512]{2,1,0:T(8,128)} %param.15) | copy-start | bytes 6291460
  200.4 1.9 copy-start.4
  202.3 4.1 %copy-start.1 = (f32[512,512]{1,0:T(8,128)}, f32[512,512]{1,0:T(8,128)S(1)}, u32[]{:S(2)}) copy-start(f32[512,512]{1,0:T(8,128)S(1)} %fusion.29) | copy-start | bytes 3145732
  224.3 61.1 %all-to-all-start.1 = ((bf16[128,32,512]{2,1,0:T(8,128)(2,1)}), bf16[128,32,512]{2,1,0:T(8,128)(2,1)}, u32[]{:S(2)}, u32[]{:S(2)}) async-start(bf16[128,32,512]{2,1,0:T(8,128)(2,1)} %select_dynamic-update-slice_fusion), calls=%async_computation.1 | async-start | bytes 8388608 | tf_op jit(solution)/shard_map/all_to_all | solution.py:115
  238.9 2.3 copy-start.7
  246.4 2.4 copy-start.3
where the time goes:
time: 293 us; the launch traced here: 289 us
  waiting for transfers between devices  129 us (44%)
  blocking collectives  68.2 us (23%)
  matrix products  33.8 us (12%)
  local copies, waits for them, and re-layouts  18.2 us (6%)
  other arithmetic  18.1 us (6%)
  starting transfers between devices  14.9 us (5%)
  between operations  7.08 us (2%)
    all_to_all x1, waiting for transfers between devices, per_device(): lax.all_to_all(sendbuf, 'dp', split_axis=0, concat_axis=0, tiled=True)  99 us
    psum x1, blocking collectives, clip_scale(): summed = lax.psum(squares, 'dp')  68.2 us
    dot_general x12, matrix products, matmul_full(): return jnp.dot(left_arr, right_arr, precision=full_precision)  33.8 us
    all_to_all x1, waiting for transfers between devices, per_device(): lax.all_to_all(backbuf, 'dp', split_axis=0, concat_axis=0, tiled=True)  30.1 us
    another operation x5, other arithmetic, per_device(): jnp.stack([jnp.where(present[slot_index], results[slot_index][state_pos],...  10.5 us
    all_to_all x1, starting transfers between devices, per_device(): lax.all_to_all(backbuf, 'dp', split_axis=0, concat_axis=0, tiled=True)  8.49 us
    all_to_all x1, starting transfers between devices, per_device(): lax.all_to_all(sendbuf, 'dp', split_axis=0, concat_axis=0, tiled=True)  6.39 us
  transfers between devices with their start and end apart: 2, of which 2 were waited for; matrix products, arithmetic and copies ran while one was open for 8% of the time, Pallas kernels for 0%

commit v1 on v0

v1 whole, which is shorter than its diff:
```python
import jax
import jax.numpy as jnp
from jax import lax
from jax.experimental import pallas as pl
from jax.experimental.pallas import tpu as pltpu
from jax.sharding import PartitionSpec as P

MESH = pl.DeviceIdType.MESH
N = 128


def shift_peer(me, k):
    x, z, y, c = me // 32, (me // 8) % 4, (me // 2) % 4, me % 2
    dx, dz, dy, dc = k % 4, (k // 4) % 4, (k // 16) % 4, k // 64
    return ((x + dx) % 4) * 32 + ((z + dz) % 4) * 8 + ((y + dy) % 4) * 2 + (c + dc) % 2


def enter(me):
    barrier = pltpu.get_barrier_semaphore()

    def hail(k, carry):
        pl.semaphore_signal(barrier, inc=1, device_id=(shift_peer(me, k),), device_id_type=MESH)
        return carry

    lax.fori_loop(1, N, hail, 0)
    return barrier


def forward_kernel(index_ref, grad_ref, out_ref, send1, recv1, send2, sems):
    me = lax.axis_index("dp")
    group, rank = me // 16, me % 16
    half, part = group // 4, group % 4
    barrier = enter(me)
    for h in range(2):
        for j in range(4):
            for c in range(16):
                send1[h * 4 + j, c] = grad_ref[16 * h:16 * h + 16, 512 * c + 128 * j:512 * c + 128 * j + 128]
    pl.semaphore_wait(barrier, N - 1)

    def spread(d, carry):
        to = (group + d) % 8
        pltpu.make_async_remote_copy(
            src_ref=send1.at[to], dst_ref=recv1.at[group], send_sem=sems.at[0], recv_sem=sems.at[1],
            device_id=(to * 16 + rank,), device_id_type=MESH).start()
        return carry

    lax.fori_loop(1, 8, spread, 0)
    pltpu.make_async_copy(send1.at[group], recv1.at[group], sems.at[1]).start()
    pltpu.make_async_copy(recv1, recv1, sems.at[1]).wait()

    def pack(o):
        for s in range(2):
            b = index_ref[2 * o + s]
            send2[o, s] = recv1[b // 16, b % 16]

    row = pl.multiple_of(32 * rank + 16 * half, 16)
    col = pl.multiple_of(128 * part, 128)
    place = out_ref.at[:, pl.ds(row, 16), pl.ds(col, 128)]

    def deliver(k, carry):
        o = shift_peer(me, k)
        pack(o)
        pltpu.make_async_remote_copy(
            src_ref=send2.at[o], dst_ref=place, send_sem=sems.at[2], recv_sem=sems.at[3],
            device_id=(o,), device_id_type=MESH).start()
        return carry

    lax.fori_loop(1, N, deliver, 0)
    pack(me)
    pltpu.make_async_copy(send2.at[me], place, sems.at[3]).start()
    pltpu.make_async_copy(out_ref, out_ref, sems.at[3]).wait()
    pltpu.make_async_copy(send1.at[pl.ds(0, 7)], send1.at[pl.ds(0, 7)], sems.at[0]).wait()
    pltpu.make_async_copy(send2.at[pl.ds(0, N - 1)], send2.at[pl.ds(0, N - 1)], sems.at[2]).wait()


def forward(index, grad):
    dt = grad.dtype
    return pl.pallas_call(
        forward_kernel,
        out_shape=jax.ShapeDtypeStruct((2, 512, 512), dt),
        in_specs=[pl.BlockSpec(memory_space=pltpu.SMEM), pl.BlockSpec(memory_space=pltpu.VMEM)],
        out_specs=pl.BlockSpec(memory_space=pltpu.VMEM),
        scratch_shapes=[
            pltpu.VMEM((8, 16, 16, 128), dt),
            pltpu.VMEM((8, 16, 16, 128), dt),
            pltpu.VMEM((N, 2, 16, 128), dt),
            pltpu.SemaphoreType.DMA((4,)),
        ],
        compiler_params=pltpu.CompilerParams(
            collective_id=0, has_side_effects=True, vmem_limit_bytes=40 * 2**20),
        name="forward_rows",
    )(index, grad)


def back_kernel(index_ref, upd_ref, out_ref, recv2, send1, recv1, sems):
    me = lax.axis_index("dp")
    group, rank = me // 16, me % 16
    barrier = enter(me)
    pl.semaphore_wait(barrier, N - 1)

    def place(i):
        g = i // 16
        row = pl.multiple_of(32 * (i % 16) + 16 * (g // 4), 16)
        col = pl.multiple_of(128 * (g % 4), 128)
        return upd_ref.at[:, pl.ds(row, 16), pl.ds(col, 128)]

    def deliver(k, carry):
        o = shift_peer(me, k)
        pltpu.make_async_remote_copy(
            src_ref=place(o), dst_ref=recv2.at[me], send_sem=sems.at[0], recv_sem=sems.at[1],
            device_id=(o,), device_id_type=MESH).start()
        return carry

    lax.fori_loop(1, N, deliver, 0)
    pltpu.make_async_copy(place(me), recv2.at[me], sems.at[1]).start()
    pltpu.make_async_copy(recv2, recv2, sems.at[1]).wait()

    def pack(g):
        for c in range(16):
            q = index_ref[16 * g + c]
            send1[g, c] = recv2[q // 2, q % 2]

    def spread(d, carry):
        to = (group + d) % 8
        pack(to)
        pltpu.make_async_remote_copy(
            src_ref=send1.at[to], dst_ref=recv1.at[group], send_sem=sems.at[2], recv_sem=sems.at[3],
            device_id=(to * 16 + rank,), device_id_type=MESH).start()
        return carry

    lax.fori_loop(1, 8, spread, 0)
    pack(group)
    pltpu.make_async_copy(send1.at[group], recv1.at[group], sems.at[3]).start()
    pltpu.make_async_copy(recv1, recv1, sems.at[3]).wait()
    for h in range(2):
        for j in range(4):
            for c in range(16):
                out_ref[16 * h:16 * h + 16, 512 * c + 128 * j:512 * c + 128 * j + 128] = recv1[h * 4 + j, c]
    pltpu.make_async_copy(recv2.at[pl.ds(0, N - 1)], recv2.at[pl.ds(0, N - 1)], sems.at[0]).wait()
    pltpu.make_async_copy(send1.at[pl.ds(0, 7)], send1.at[pl.ds(0, 7)], sems.at[2]).wait()


def back(index, upd):
    dt = upd.dtype
    return pl.pallas_call(
        back_kernel,
        out_shape=jax.ShapeDtypeStruct((32, 8192), dt),
        in_specs=[pl.BlockSpec(memory_space=pltpu.SMEM), pl.BlockSpec(memory_space=pltpu.VMEM)],
        out_specs=pl.BlockSpec(memory_space=pltpu.VMEM),
        scratch_shapes=[
            pltpu.VMEM((N, 2, 16, 128), dt),
            pltpu.VMEM((8, 16, 16, 128), dt),
            pltpu.VMEM((8, 16, 16, 128), dt),
            pltpu.SemaphoreType.DMA((4,)),
        ],
        compiler_params=pltpu.CompilerParams(
            collective_id=1, has_side_effects=True, vmem_limit_bytes=40 * 2**20),
        name="back_rows",
    )(index, upd)


def matmul_full(left_arr, right_arr):
    return jnp.dot(left_arr, right_arr, precision=lax.Precision.HIGHEST)


def block_slots(block_owner):
    positions = jnp.arange(block_owner.shape[0], dtype=jnp.int32)
    same_owner = block_owner[:, None] == block_owner[None, :]
    earlier = positions[None, :] < positions[:, None]
    return jnp.sum(jnp.where(same_owner & earlier, 1, 0), axis=1).astype(jnp.int32)


def soap_block(grad_block, left_stat, right_stat, left_rot, right_rot, first_stat, second_stat):
    next_left = 0.95 * left_stat + 0.05 * matmul_full(grad_block, grad_block.T)
    next_right = 0.95 * right_stat + 0.05 * matmul_full(grad_block.T, grad_block)
    rotated = matmul_full(matmul_full(left_rot.T, grad_block), right_rot)
    next_first = 0.9 * first_stat + 0.1 * rotated
    next_second = 0.95 * second_stat + 0.05 * rotated * rotated
    direction = next_first / (1.0 - 0.9**10) / (jnp.sqrt(next_second / (1.0 - 0.95**10)) + 1e-08)
    update = matmul_full(matmul_full(left_rot, direction), right_rot.T).astype(jnp.bfloat16)
    return (next_left, next_right, next_first, next_second, update)


def per_device(grad, block_owner, left_factor, right_factor, left_basis, right_basis, first_moment, second_moment):
    me = lax.axis_index("dp")
    place = 2 * block_owner + block_slots(block_owner)
    hits = place[None, :] == jnp.arange(2 * N, dtype=jnp.int32)[:, None]
    index = jnp.sum(jnp.where(hits, jnp.arange(N, dtype=jnp.int32)[None, :], 0), axis=1)
    filled = jnp.any(hits, axis=1)
    squares = lax.psum(jnp.sum(grad * grad), "dp")
    scale = jnp.minimum(1.0, 0.04 / (jnp.sqrt(squares / (N * grad.size)) + 1e-06))
    blocks = forward(index, grad) * scale
    results = [
        soap_block(blocks[s], left_factor[s], right_factor[s], left_basis[s], right_basis[s], first_moment[s], second_moment[s])
        for s in range(2)
    ]
    mine = lax.dynamic_slice_in_dim(filled, 2 * me, 2, 0)
    olds = (left_factor, right_factor, first_moment, second_moment)
    news = [
        jnp.stack([jnp.where(mine[s], results[s][t], olds[t][s]) for s in range(2)])
        for t in range(4)
    ]
    updates = back(place, jnp.stack([results[s][4] for s in range(2)]))
    return (updates, *news)


def solution(mesh):
    rows, state = P("dp", None), P("dp", None, None)
    return jax.shard_map(
        per_device, mesh=mesh, in_specs=(rows, P()) + (state,) * 6,
        out_specs=(rows,) + (state,) * 4, check_vma=False,
    )
```

time: 293 us -> 213 us (0.73)
  waiting for transfers between devices: 129 us -> 0 us
  Pallas kernels: 0 us -> 93.4 us
  starting transfers between devices: 14.9 us -> 0 us
  local copies, waits for them, and re-layouts: 18.2 us -> 4.07 us
  other arithmetic: 18.1 us -> 11.2 us
  between operations: 7.08 us -> 1.6 us
    all_to_all x2 -> x0, waiting for transfers between devices: 129 us -> none  [the longest x1 99 us: per_device(): lax.all_to_all(sendbuf, 'dp', split_axis=0, concat_axis=0, tiled=True)]
    pallas_call x0 -> x2, Pallas kernels: none -> 93.4 us  [the longest x1 54.6 us: forward(): pl.pallas_call(forward_kernel, out_shape=jax.ShapeDtypeStruct((2, 512, 51...]
    all_to_all x2 -> x0, starting transfers between devices: 14.9 us -> none  [the longest x1 8.49 us: per_device(): lax.all_to_all(backbuf, 'dp', split_axis=0, concat_axis=0, tiled=True)]
    broadcast_in_dim x2 -> x0, local copies, waits for them, and re-layouts: 6.78 us -> none  [the longest x1 4.28 us: per_device(): jnp.zeros((devices, dev_rows, block_order), jnp.float32).at[row_owner]]
    another operation x5 -> x4, other arithmetic: 10.5 us -> 7.12 us  [the longest x3 7.02 us: per_device(): jnp.stack([jnp.where(mine[s], results[s][t], olds[t][s]) for s in range(2)])]
    scatter x1 -> x0, local copies, waits for them, and re-layouts: 2.95 us -> none  [per_device(): jnp.zeros((devices, dev_rows, block_order), jnp.float32).at[row_owner]]
  transfers between devices with their start and end apart: 2 -> 0, of which waited for: 2 -> 0; matrix products, arithmetic and copies ran while one was open for 8% -> 0% of each run, Pallas kernels for 0% -> 0%
where the time goes in v1:
time: 213 us; the launch traced here: 212 us
  Pallas kernels  93.4 us (44%)
  blocking collectives  68.2 us (32%)
  matrix products  33.5 us (16%)
  other arithmetic  11.2 us (5%)
  local copies, waits for them, and re-layouts  4.07 us (2%)
    psum x1, blocking collectives, per_device(): squares = lax.psum(jnp.sum(grad * grad), 'dp')  68.2 us
    pallas_call x1, Pallas kernels, forward(): pl.pallas_call(forward_kernel, out_shape=jax.ShapeDtypeStruct((2, 512, 51...  54.6 us
    pallas_call x1, Pallas kernels, back(): pl.pallas_call(back_kernel, out_shape=jax.ShapeDtypeStruct((32, 8192), dt...  38.7 us
    dot_general x12, matrix products, matmul_full(): return jnp.dot(left_arr, right_arr, precision=lax.Precision.HIGHEST)  33.5 us
    another operation x3, other arithmetic, per_device(): jnp.stack([jnp.where(mine[s], results[s][t], olds[t][s]) for s in range(2)])  7.02 us

profile of v1, /device:TPU:0, one launch (start us, length us, event | category | flops | bytes accessed | tf_op | source)
XLA Modules:
  0.0 211.9 jit_solution(8558304558218234429)
XLA Ops:
  0.6 2.1 multiply_reduce_fusion
  2.7 68.2 %psum.7 = f32[]{:T(128)} all-reduce(f32[]{:T(128)} %multiply_reduce_fusion), channel_id=1, replica_groups=mesh['dp'=128] {'dp'}, use_global_device_ids=true, to_apply=%region_3.4 | all-reduce | flops 1 | bytes 8 | tf_op jit(solution)/shard_map/psum | solution.py:190
  71.7 0.9 select_reduce_fusion.1
  72.6 0.7 multiply_add_fusion.index_ref
  74.1 1.2 copy-done
  75.4 54.6 %forward_rows.1 = f32[2,512,512]{2,1,0:T(8,128)S(1)} custom-call(s32[256]{0:T(256)S(1)} %select_reduce_fusion.index_ref, f32[32,8192]{1,0:T(8,128)S(1)} %copy-done), custom_call_target="tpu_custom_call" | custom-call | tf_op jit(solution)/shard_map/forward_rows/pallas_call | solution.py:78
  130.2 1.3 copy-done.3
  131.6 2.7 %fusion.7 = f32[1,512,512]{2,1,0:T(8,128)S(1)} fusion(f32[2,512,512]{2,1,0:T(8,128)S(1)} %copy-done.3, f32[2,512,512]{2,1,0:T(8,128)S(1)} %broadcast_multiply_fusion, pred[]{:T(512)} %bitcast.15), kind=kOutput, calls=%fused_computation.17 | convolution fusion | flops 1611661312 | bytes 3145729 | tf_op jit(solution)/shard_map/dot_general | solution.py:163
  134.3 2.6 %fusion.11 = f32[1,512,512]{2,1,0:T(8,128)S(1)} fusion(f32[2,512,512]{2,1,0:T(8,128)S(1)} %copy-done.4, f32[2,512,512]{2,1,0:T(8,128)S(1)} %broadcast_multiply_fusion, pred[]{:T(512)} %bitcast.15), kind=kOutput, calls=%fused_computation.21 | convolution fusion | flops 1611661312 | bytes 3145729 | tf_op jit(solution)/shard_map/dot_general | solution.py:163
  136.9 2.6 %fusion.5 = f32[1,512,512]{2,1,0:T(8,128)S(1)} fusion(f32[2,512,512]{2,1,0:T(8,128)S(1)} %copy-done.3, f32[2,512,512]{2,1,0:T(8,128)S(1)} %broadcast_multiply_fusion, pred[]{:T(512)} %bitcast.12), kind=kOutput, calls=%fused_computation.15 | convolution fusion | flops 1611661312 | bytes 3145729 | tf_op jit(solution)/shard_map/dot_general | solution.py:163
  139.5 2.5 %fusion.9 = f32[1,512,512]{2,1,0:T(8,128)S(1)} fusion(f32[2,512,512]{2,1,0:T(8,128)S(1)} %copy-done.4, f32[2,512,512]{2,1,0:T(8,128)S(1)} %broadcast_multiply_fusion, pred[]{:T(512)} %bitcast.12), kind=kOutput, calls=%fused_computation.19 | convolution fusion | flops 1611661312 | bytes 3145729 | tf_op jit(solution)/shard_map/dot_general | solution.py:163
  142.1 2.5 %pad_maximum_fusion = (f32[2,512,512]{2,1,0:T(8,128)}, f32[2,512,512]{2,1,0:T(8,128)}) fusion(f32[1,512,512]{2,1,0:T(8,128)S(1)} %fusion.7, f32[1,512,512]{2,1,0:T(8,128)S(1)} %fusion.5, f32[1,512,512]{2,1,0:T(8,128)S(1)} %fusion.11, f32[1,512,512]{2,1,0:T(8,128)S(1)} %fusion.9), kind=kLoop, calls=%fused_computation | loop fusion | flops 1048576 | bytes 8388608 | tf_op jit(solution)/shard_map/stack | solution.py:200
  144.5 1.8 fusion.22
  146.4 2.0 fusion.32
  148.5 1.9 fusion.28
  150.4 1.9 fusion.18
  152.3 4.1 %fusion.20 = f32[512,512]{1,0:T(8,128)S(1)} fusion(f32[2,512,512]{2,1,0:T(8,128)S(1)} %copy-done.2, f32[512,512]{1,0:T(8,128)S(1)} %fusion.18, f32[2,512,512]{2,1,0:T(8,128)S(1)} %copy-done.5, f32[2,512,512]{2,1,0:T(8,128)S(1)} %copy-done.6), kind=kOutput, calls=%fused_computation.41 | convolution fusion | flops 1613496320 | bytes 5242880 | tf_op jit(solution)/shard_map/dot_general | solution.py:163
  156.4 3.5 %fusion.13 = bf16[1,512,512]{2,1,0:T(8,128)(2,1)S(1)} fusion(f32[512,512]{1,0:T(8,128)S(1)} %fusion.20, f32[2,512,512]{2,1,0:T(8,128)S(1)} %copy-done.1), kind=kOutput, calls=%fused_computation.25 | convolution fusion | flops 1610874880 | bytes 2621440 | tf_op jit(solution)/shard_map/dot_general | solution.py:163
  159.9 4.3 %fusion.30 = f32[512,512]{1,0:T(8,128)S(1)} fusion(f32[2,512,512]{2,1,0:T(8,128)S(1)} %copy-done.2, f32[512,512]{1,0:T(8,128)S(1)} %fusion.28, f32[2,512,512]{2,1,0:T(8,128)S(1)} %copy-done.5, f32[2,512,512]{2,1,0:T(8,128)S(1)} %copy-done.6), kind=kOutput, calls=%fused_computation.55 | convolution fusion | flops 1613496320 | bytes 5242880 | tf_op jit(solution)/shard_map/dot_general | solution.py:163
  164.2 3.5 %fusion.12 = bf16[1,512,512]{2,1,0:T(8,128)(2,1)S(1)} fusion(f32[512,512]{1,0:T(8,128)S(1)} %fusion.30, f32[2,512,512]{2,1,0:T(8,128)S(1)} %copy-done.1), kind=kOutput, calls=%fused_computation.24 | convolution fusion | flops 1610874880 | bytes 2621440 | tf_op jit(solution)/shard_map/dot_general | solution.py:163
  167.8 38.7 %back_rows.1 = bf16[32,8192]{1,0:T(8,128)(2,1)S(1)} custom-call(s32[128]{0:T(128)S(1)} %multiply_add_fusion.index_ref, bf16[2,512,512]{2,1,0:T(8,128)(2,1)S(1)} %pad_maximum_fusion.4.upd_ref), custom_call_target="tpu_custom_call" | custom-call | tf_op jit(solution)/shard_map/back_rows/pallas_call | solution.py:145
  206.6 2.1 fusion.35
  208.7 2.5 %pad_maximum_fusion.2 = (f32[2,512,512]{2,1,0:T(8,128)}, f32[2,512,512]{2,1,0:T(8,128)}) fusion(f32[1,512,512]{2,1,0:T(8,128)S(1)} %get-tuple-element.8, f32[1,512,512]{2,1,0:T(8,128)S(1)} %get-tuple-element.7, f32[1,512,512]{2,1,0:T(8,128)S(1)} %get-tuple-element.9, f32[1,512,512]{2,1,0:T(8,128)S(1)} %get-tuple-element.10), kind=kLoop, calls=%fused_computation.2 | loop fusion | flops 1048576 | bytes 8388608 | tf_op jit(solution)/shard_map/stack | solution.py:200
  211.1 0.8 copy.14
  (18 shorter events, 1.3 us)
Async XLA Ops:
  74.1 1.2 copy-start
  130.0 1.6 copy-start.3
  131.6 2.7 %copy-start.4 = (f32[2,512,512]{2,1,0:T(8,128)S(1)}, f32[2,512,512]{2,1,0:T(8,128)}, u32[]{:S(2)}) copy-start(f32[2,512,512]{2,1,0:T(8,128)} %param.11) | copy-start | bytes 6291460
  142.1 2.5 %copy-start.2 = (f32[2,512,512]{2,1,0:T(8,128)S(1)}, f32[2,512,512]{2,1,0:T(8,128)}, u32[]{:S(2)}) copy-start(f32[2,512,512]{2,1,0:T(8,128)} %param.12) | copy-start | bytes 6291460
  146.4 2.1 copy-start.1
  148.5 3.8 %copy-start.6 = (f32[2,512,512]{2,1,0:T(8,128)S(1)}, f32[2,512,512]{2,1,0:T(8,128)}, u32[]{:S(2)}) copy-start(f32[2,512,512]{2,1,0:T(8,128)} %param.15) | copy-start | bytes 6291460
  150.4 1.9 copy-start.5

commit v2 on v0

v2 whole, which is shorter than its diff:
```python
import jax
import jax.numpy as jnp
from jax import lax
from jax.experimental import pallas as pl
from jax.experimental.pallas import tpu as pltpu
from jax.sharding import PartitionSpec as P

MESH = pl.DeviceIdType.MESH
N = 128
GROUPS = 8
RANKS = 16
ORDER = 512
STRIDE = 45
UNROLL = 8
LEVELS = 32767.0
FIRST_CORRECTION = 1.0 - 0.9**10
SECOND_CORRECTION = 1.0 - 0.95**10
f32, bf16, i32, i16 = jnp.float32, jnp.bfloat16, jnp.int32, jnp.int16


def split(x):
    high = x.astype(bf16)
    return high, (x - high.astype(f32)).astype(bf16)


def product(left, right, contract):
    def one(a, b):
        return lax.dot_general(a, b, (contract, ((), ())), preferred_element_type=f32)

    (lh, ll), (rh, rl) = left, right
    return one(lh, rh) + one(lh, rl) + one(ll, rh)


def each_peer(me, act):
    def step(_, cur):
        cur = lax.rem(cur + STRIDE, N)
        act(cur)
        return cur

    lax.fori_loop(1, N, step, me, unroll=UNROLL)


def remote(src, dst, send_sem, recv_sem, peer):
    pltpu.make_async_remote_copy(
        src_ref=src, dst_ref=dst, send_sem=send_sem, recv_sem=recv_sem, device_id=(peer,), device_id_type=MESH).start()


def arrive(ref, sem):
    pltpu.make_async_copy(ref, ref, sem).wait()


def step_kernel(
    table, grad, left_basis, right_basis, first, second, left, right,
    updates, new_left, new_right, new_first, new_second,
    grad_v, basis_v, old_v, basis_s, note, notes, send1, recv1, send2, land, grad_s, work_s, back, recv3, send4, recv4,
    loads, sends, recvs,
):
    me = lax.axis_index("dp")
    group, rank = me // RANKS, me % RANKS
    half, part = group // 4, group % 4

    pairs = [(grad, grad_v), (left_basis, basis_v.at[0]), (right_basis, basis_v.at[1]), (first, old_v.at[0]),
             (second, old_v.at[1]), (left, old_v.at[2]), (right, old_v.at[3])]
    copies = [pltpu.make_async_copy(src, dst, loads.at[k]) for k, (src, dst) in enumerate(pairs)]
    for copy in copies:
        copy.start()
    barrier = pltpu.get_barrier_semaphore()
    each_peer(me, lambda peer: pl.semaphore_signal(barrier, inc=1, device_id=(peer,), device_id_type=MESH))

    copies[0].wait()
    values = grad_v[...]
    top = jnp.max(jnp.abs(values), axis=1, keepdims=True)
    squares = jnp.sum(values * values)
    inverse = jnp.where(top > 1e-37, 1.0 / jnp.maximum(top, 1e-37), 0.0)
    row = lax.broadcasted_iota(i32, (32, 128), 0)
    lane = lax.broadcasted_iota(i32, (32, 128), 1)
    tops = jnp.sum(jnp.where(lane == row, top, 0.0), axis=0, keepdims=True)
    note[...] = tops + jnp.where(lane[:1] == 32, squares, 0.0)

    def encode(c, carry):
        for h in range(2):
            for j in range(4):
                col = pl.multiple_of(ORDER * c + 128 * j, 128)
                tile = grad_v[16 * h:16 * h + 16, pl.ds(col, 128)]
                code = (jnp.sqrt(jnp.abs(tile) * inverse[16 * h:16 * h + 16]) * LEVELS + 0.5).astype(i32)
                send1[4 * h + j, c] = jnp.where(tile < 0.0, -code, code).astype(i16)
        return carry

    lax.fori_loop(0, RANKS, encode, 0)
    pl.semaphore_wait(barrier, N - 1)

    for d in range(1, GROUPS):
        to = lax.rem(group + d, GROUPS)
        remote(send1.at[to], recv1.at[group], sends.at[0], recvs.at[0], to * RANKS + rank)
    pltpu.make_async_copy(send1.at[group], recv1.at[group], recvs.at[0]).start()
    each_peer(me, lambda peer: remote(note, notes.at[me], sends.at[1], recvs.at[1], peer))
    pltpu.make_async_copy(note, notes.at[me], recvs.at[1]).start()

    for k in range(2):
        copies[1 + k].wait()
        for s in range(2):
            basis_s[k, s, 0], basis_s[k, s, 1] = split(basis_v[k, s])
    arrive(recv1, recvs.at[0])

    at_row = pl.multiple_of(32 * rank + 16 * half, 16)
    at_col = pl.multiple_of(128 * part, 128)

    def deliver(s, carry):
        place = land.at[s, pl.ds(at_row, 16), pl.ds(at_col, 128)]

        def pack(peer):
            block = table[2 * peer + s]
            send2[s, peer] = recv1[block // RANKS, block % RANKS]

        def post(peer):
            pack(peer)
            remote(send2.at[s, peer], place, sends.at[2], recvs.at[2 + s], peer)

        each_peer(me, post)
        pack(me)
        pltpu.make_async_copy(send2.at[s, me], place, recvs.at[2 + s]).start()
        return carry

    lax.fori_loop(0, 2, deliver, 0)

    arrive(notes, recvs.at[1])
    lanes = lax.broadcasted_iota(i32, (1, 128), 1)
    total = jnp.sum(jnp.where(lanes == 32, jnp.sum(notes[...], axis=0), 0.0), axis=1, keepdims=True)
    scale = jnp.minimum(1.0, 0.04 / (jnp.sqrt(total / (N * 32 * 8192)) + 1e-06))
    for copy in copies[3:]:
        copy.wait()

    def compute(s, carry):
        arrive(land.at[s], recvs.at[2 + s])
        from_group = table[2 * me + s] // RANKS

        def decode(d, inner):
            rows = pl.ds(pl.multiple_of(32 * d, 32), 32)
            tops = notes[from_group * RANKS + d] * scale
            factor = jnp.sum(jnp.where(lane == row, tops, 0.0), axis=1, keepdims=True)
            code = land[s, rows, :].astype(i32).astype(f32) * (1.0 / LEVELS)
            high, low = split(code * jnp.abs(code) * factor)
            grad_s[s, 0, rows, :] = high
            grad_s[s, 1, rows, :] = low
            return inner

        lax.fori_loop(0, RANKS, decode, 0)
        lh, ll, rh, rl = basis_s[0, s, 0], basis_s[0, s, 1], basis_s[1, s, 0], basis_s[1, s, 1]
        half_turned = product((lh, ll), (grad_s[s, 0], grad_s[s, 1]), ((0,), (0,)))
        work_s[0], work_s[1] = split(half_turned)
        turned = product((work_s[0], work_s[1]), (rh, rl), ((1,), (0,)))
        kept = table[2 * N + 2 * me + s] > 0
        moved = jnp.where(kept, 0.9, 1.0) * old_v[0, s] + jnp.where(kept, 0.1, 0.0) * turned
        spread = jnp.where(kept, 0.95, 1.0) * old_v[1, s] + jnp.where(kept, 0.05, 0.0) * turned * turned
        new_first[s] = moved
        new_second[s] = spread
        direction = moved / FIRST_CORRECTION / (jnp.sqrt(spread / SECOND_CORRECTION) + 1e-08)
        work_s[0], work_s[1] = split(direction)
        half_back = product((lh, ll), (work_s[0], work_s[1]), ((1,), (0,)))
        work_s[0], work_s[1] = split(half_back)
        back[s] = product((work_s[0], work_s[1]), (rh, rl), ((1,), (1,))).astype(bf16)

        def place(peer):
            peer_row = pl.multiple_of(32 * (peer % RANKS) + 16 * (peer // 64), 16)
            peer_col = pl.multiple_of(128 * ((peer // RANKS) % 4), 128)
            return back.at[s, pl.ds(peer_row, 16), pl.ds(peer_col, 128)]

        each_peer(me, lambda peer: remote(place(peer), recv3.at[s, me], sends.at[3], recvs.at[4], peer))
        pltpu.make_async_copy(place(me), recv3.at[s, me], recvs.at[4]).start()
        return carry

    lax.fori_loop(0, 2, compute, 0)

    def factors(s, carry):
        kept = table[2 * N + 2 * me + s] > 0
        stay, fresh = jnp.where(kept, 0.95, 1.0), jnp.where(kept, 0.05, 0.0)
        halves = (grad_s[s, 0], grad_s[s, 1])
        new_left[s] = stay * old_v[2, s] + fresh * product(halves, halves, ((1,), (1,)))
        new_right[s] = stay * old_v[3, s] + fresh * product(halves, halves, ((0,), (0,)))
        return carry

    lax.fori_loop(0, 2, factors, 0)

    arrive(recv3, recvs.at[4])

    def collect(g):
        for c in range(RANKS):
            slot = table[4 * N + RANKS * g + c]
            send4[g, c] = recv3[slot % 2, slot // 2]

    for d in range(1, GROUPS):
        to = lax.rem(group + d, GROUPS)
        collect(to)
        remote(send4.at[to], recv4.at[group], sends.at[4], recvs.at[5], to * RANKS + rank)
    collect(group)
    pltpu.make_async_copy(send4.at[group], recv4.at[group], recvs.at[5]).start()
    arrive(recv4, recvs.at[5])

    def unpack(c, carry):
        for h in range(2):
            for j in range(4):
                col = pl.multiple_of(ORDER * c + 128 * j, 128)
                updates[16 * h:16 * h + 16, pl.ds(col, 128)] = recv4[4 * h + j, c]
        return carry

    lax.fori_loop(0, RANKS, unpack, 0)
    others = pl.ds(0, N - 1)
    arrive(send1.at[pl.ds(0, GROUPS - 1)], sends.at[0])
    arrive(notes.at[others], sends.at[1])
    arrive(send4.at[pl.ds(0, GROUPS - 1)], sends.at[4])
    for s in range(2):
        arrive(send2.at[s, others], sends.at[2])
        arrive(recv3.at[s, others], sends.at[3])


def block_slots(block_owner):
    positions = jnp.arange(block_owner.shape[0], dtype=i32)
    same_owner = block_owner[:, None] == block_owner[None, :]
    earlier = positions[None, :] < positions[:, None]
    return jnp.sum(jnp.where(same_owner & earlier, 1, 0), axis=1).astype(i32)


def per_device(grad, block_owner, left_factor, right_factor, left_basis, right_basis, first_moment, second_moment):
    place = 2 * block_owner + block_slots(block_owner)
    hits = place[None, :] == jnp.arange(2 * N, dtype=i32)[:, None]
    index = jnp.sum(jnp.where(hits, jnp.arange(N, dtype=i32)[None, :], 0), axis=1)
    table = jnp.concatenate([index, jnp.any(hits, axis=1).astype(i32), place])
    state = pltpu.VMEM((2, ORDER, ORDER), f32)
    in_hbm = pl.BlockSpec(memory_space=pl.ANY)
    in_vmem = pl.BlockSpec(memory_space=pltpu.VMEM)
    return pl.pallas_call(
        step_kernel,
        out_shape=[pltpu.VMEM(grad.shape, bf16)] + [state] * 4,
        in_specs=[pl.BlockSpec(memory_space=pltpu.SMEM)] + [in_hbm] * 7,
        out_specs=[in_vmem] * 5,
        scratch_shapes=[
            pltpu.VMEM(grad.shape, f32),
            pltpu.VMEM((2, 2, ORDER, ORDER), f32),
            pltpu.VMEM((4, 2, ORDER, ORDER), f32),
            pltpu.VMEM((2, 2, 2, ORDER, ORDER), bf16),
            pltpu.VMEM((1, 128), f32),
            pltpu.VMEM((N, 1, 128), f32),
            pltpu.VMEM((GROUPS, RANKS, 16, 128), i16),
            pltpu.VMEM((GROUPS, RANKS, 16, 128), i16),
            pltpu.VMEM((2, N, 16, 128), i16),
            pltpu.VMEM((2, ORDER, ORDER), i16),
            pltpu.VMEM((2, 2, ORDER, ORDER), bf16),
            pltpu.VMEM((2, ORDER, ORDER), bf16),
            pltpu.VMEM((2, ORDER, ORDER), bf16),
            pltpu.VMEM((2, N, 16, 128), bf16),
            pltpu.VMEM((GROUPS, RANKS, 16, 128), bf16),
            pltpu.VMEM((GROUPS, RANKS, 16, 128), bf16),
            pltpu.SemaphoreType.DMA((7,)),
            pltpu.SemaphoreType.DMA((5,)),
            pltpu.SemaphoreType.DMA((6,)),
        ],
        compiler_params=pltpu.CompilerParams(
            collective_id=0, has_side_effects=True, vmem_limit_bytes=50 * 2**20),
        name="soap_step",
    )(table, grad, left_basis, right_basis, first_moment, second_moment, left_factor, right_factor)


def solution(mesh):
    rows, state = P("dp", None), P("dp", None, None)
    return jax.shard_map(
        per_device, mesh=mesh, in_specs=(rows, P()) + (state,) * 6,
        out_specs=(rows,) + (state,) * 4, check_vma=False,
    )
```

time: 293 us -> 73.9 us (0.25); the launches traced: 289 us -> 73.8 us
  waiting for transfers between devices: 129 us -> 0 us
  blocking collectives: 68.2 us -> 0 us
  Pallas kernels: 0 us -> 64.6 us
  matrix products: 33.8 us -> 0 us
  other arithmetic: 18.1 us -> 2.41 us
  starting transfers between devices: 14.9 us -> 0 us
  local copies, waits for them, and re-layouts: 18.2 us -> 6.07 us
  between operations: 7.08 us -> 0.65 us
    all_to_all x2 -> x0, waiting for transfers between devices: 129 us -> none  [the longest x1 99 us: per_device(): lax.all_to_all(sendbuf, 'dp', split_axis=0, concat_axis=0, tiled=True)]
    psum x1 -> x0, blocking collectives: 68.2 us -> none  [clip_scale(): summed = lax.psum(squares, 'dp')]
    pallas_call x0 -> x1, Pallas kernels: none -> 64.6 us  [per_device(): pl.pallas_call(step_kernel, out_shape=[pltpu.VMEM(grad.shape, bf16)] + [s...]
    dot_general x12 -> x0, matrix products: 33.8 us -> none  [matmul_full(): return jnp.dot(left_arr, right_arr, precision=full_precision)]
    all_to_all x2 -> x0, starting transfers between devices: 14.9 us -> none  [the longest x1 8.49 us: per_device(): lax.all_to_all(backbuf, 'dp', split_axis=0, concat_axis=0, tiled=True)]
    another operation x5 -> x0, other arithmetic: 10.5 us -> none  [per_device(): jnp.stack([jnp.where(present[slot_index], results[slot_index][state_pos],...]
    broadcast_in_dim x2 -> x0, local copies, waits for them, and re-layouts: 6.78 us -> none  [the longest x1 4.28 us: per_device(): jnp.zeros((devices, dev_rows, block_order), jnp.float32).at[row_owner]]
    unnamed x16 -> x5, local copies, waits for them, and re-layouts: 2.05 us -> 6.07 us
  transfers between devices with their start and end apart: 2 -> 0, of which waited for: 2 -> 0; matrix products, arithmetic and copies ran while one was open for 8% -> 0% of each run, Pallas kernels for 0% -> 0%
where the time goes in v2:
time: 73.9 us; the launch traced here: 73.8 us
  Pallas kernels  64.6 us (87%)
  local copies, waits for them, and re-layouts  6.07 us (8%)
  other arithmetic  2.41 us (3%)
    pallas_call x1, Pallas kernels, per_device(): pl.pallas_call(step_kernel, out_shape=[pltpu.VMEM(grad.shape, bf16)] + [s...  64.6 us
    unnamed x5, local copies, waits for them, and re-layouts  6.07 us

profile of v2, /device:TPU:0, one launch (start us, length us, event | category | flops | bytes accessed | tf_op | source)
XLA Modules:
  0.0 73.8 jit_solution(16753268581280107183)
XLA Ops:
  0.6 0.9 %select_reduce_fusion.1 = s32[128]{0:T(128)S(1)} fusion(s32[128]{0:T(128)} %param.9), kind=kLoop, calls=%fused_computation.3 | loop fusion | flops 81792 | bytes 1024 | tf_op jit(solution)/shard_map/reduce_sum | solution.py:220
  1.5 0.7 multiply_add_fusion
  2.2 0.1 fusion
  2.3 0.1 select_reduce_fusion
  2.4 0.6 pad_add_fusion.table
  3.1 64.6 %soap_step.1 = (bf16[32,8192]{1,0:T(8,128)(2,1)S(1)}, f32[2,512,512]{2,1,0:T(8,128)S(1)}, f32[2,512,512]{2,1,0:T(8,128)S(1)}, f32[2,512,512]{2,1,0:T(8,128)S(1)}, f32[2,512,512]{2,1,0:T(8,128)S(1)}) custom-call(s32[640]{0:T(1024)} %pad_add_fusion.table, f32[32,8192]{1,0:T(8,128)} %grad.1, f32[2,512,512]{2,1,0:T(8,128)} %left_basis.1, ...), custom_call_target="tpu_custom_call" | custom-call | tf_op jit(solution)/shard_map/soap_step/pallas_call | solution.py:231
  67.7 0.8 %copy.18 = bf16[32,8192]{1,0:T(8,128)(2,1)} copy(bf16[32,8192]{1,0:T(8,128)(2,1)S(1)} %get-tuple-element.5) | data formatting | bytes 1048576
  68.5 1.3 %copy.19 = f32[2,512,512]{2,1,0:T(8,128)} copy(f32[2,512,512]{2,1,0:T(8,128)S(1)} %get-tuple-element.6) | data formatting | bytes 4194304
  69.8 1.3 %copy.20 = f32[2,512,512]{2,1,0:T(8,128)} copy(f32[2,512,512]{2,1,0:T(8,128)S(1)} %get-tuple-element.7) | data formatting | bytes 4194304
  71.1 1.3 %copy.21 = f32[2,512,512]{2,1,0:T(8,128)} copy(f32[2,512,512]{2,1,0:T(8,128)S(1)} %get-tuple-element.8) | data formatting | bytes 4194304
  72.4 1.3 %copy.22 = f32[2,512,512]{2,1,0:T(8,128)} copy(f32[2,512,512]{2,1,0:T(8,128)S(1)} %get-tuple-element.9) | data formatting | bytes 4194304
  (1 shorter events, 0.0 us)

commit v3 on v2

--- a/solution.py
+++ b/solution.py
@@ -50,9 +50,9 @@
 
 
 def step_kernel(
-    table, grad, left_basis, right_basis, first, second, left, right,
+    owner, grad, left_basis, right_basis, first, second, left, right,
     updates, new_left, new_right, new_first, new_second,
-    grad_v, basis_v, old_v, basis_s, note, notes, send1, recv1, send2, land, grad_s, work_s, back, recv3, send4, recv4,
+    table_v, table, factor, grad_v, basis_v, old_v, basis_s, note, notes1, notes, send1, recv1, send2, land, grad_s, work_s, back, recv3, send4, recv4,
     loads, sends, recvs,
 ):
     me = lax.axis_index("dp")
@@ -66,6 +66,21 @@
         copy.start()
     barrier = pltpu.get_barrier_semaphore()
     each_peer(me, lambda peer: pl.semaphore_signal(barrier, inc=1, device_id=(peer,), device_id_type=MESH))
+
+    above = lax.broadcasted_iota(i32, (N, N), 0)
+    along = lax.broadcasted_iota(i32, (N, N), 1)
+    owners = jnp.broadcast_to(owner[...], (N, N))
+    earlier = jnp.where((owners == owners.T) & (above < along), 1, 0)
+    places = 2 * owner[...] + jnp.sum(earlier, axis=0, keepdims=True)
+    turned_places = jnp.broadcast_to(places, (N, N)).T
+    for s in range(2):
+        hits = turned_places == 2 * along + s
+        table_v[s:s + 1] = jnp.sum(jnp.where(hits, above, 0), axis=0, keepdims=True)
+        table_v[2 + s:3 + s] = jnp.sum(jnp.where(hits, 1, 0), axis=0, keepdims=True)
+    table_v[4:5] = places
+    table_v[5:8] = jnp.zeros((3, N), i32)
+    table_copy = pltpu.make_async_copy(table_v, table, loads.at[7])
+    table_copy.start()
 
     copies[0].wait()
     values = grad_v[...]
@@ -91,15 +106,17 @@
 
     for d in range(1, GROUPS):
         to = lax.rem(group + d, GROUPS)
+        remote(note, notes1.at[group], sends.at[1], recvs.at[1], to * RANKS + rank)
         remote(send1.at[to], recv1.at[group], sends.at[0], recvs.at[0], to * RANKS + rank)
+    pltpu.make_async_copy(note, notes1.at[group], recvs.at[1]).start()
     pltpu.make_async_copy(send1.at[group], recv1.at[group], recvs.at[0]).start()
-    each_peer(me, lambda peer: remote(note, notes.at[me], sends.at[1], recvs.at[1], peer))
-    pltpu.make_async_copy(note, notes.at[me], recvs.at[1]).start()
 
     for k in range(2):
         copies[1 + k].wait()
         for s in range(2):
             basis_s[k, s, 0], basis_s[k, s, 1] = split(basis_v[k, s])
+    table_copy.wait()
+    arrive(notes1, recvs.at[1])
     arrive(recv1, recvs.at[0])
 
     at_row = pl.multiple_of(32 * rank + 16 * half, 16)
@@ -109,7 +126,7 @@
         place = land.at[s, pl.ds(at_row, 16), pl.ds(at_col, 128)]
 
         def pack(peer):
-            block = table[2 * peer + s]
+            block = table[s, peer]
             send2[s, peer] = recv1[block // RANKS, block % RANKS]
 
         def post(peer):
@@ -119,37 +136,48 @@
         each_peer(me, post)
         pack(me)
         pltpu.make_async_copy(send2.at[s, me], place, recvs.at[2 + s]).start()
+
+        @pl.when(s == 0)
+        def _():
+            for d in range(1, RANKS):
+                remote(notes1, notes.at[rank], sends.at[5], recvs.at[6], group * RANKS + lax.rem(rank + d, RANKS))
+            pltpu.make_async_copy(notes1, notes.at[rank], recvs.at[6]).start()
+
         return carry
 
     lax.fori_loop(0, 2, deliver, 0)
 
-    arrive(notes, recvs.at[1])
+    arrive(notes, recvs.at[6])
     lanes = lax.broadcasted_iota(i32, (1, 128), 1)
-    total = jnp.sum(jnp.where(lanes == 32, jnp.sum(notes[...], axis=0), 0.0), axis=1, keepdims=True)
+    total = jnp.sum(jnp.where(lanes == 32, jnp.sum(notes[...], axis=(0, 1)), 0.0), axis=1, keepdims=True)
     scale = jnp.minimum(1.0, 0.04 / (jnp.sqrt(total / (N * 32 * 8192)) + 1e-06))
     for copy in copies[3:]:
         copy.wait()
 
+    for s in range(2):
+        from_group = table[s, me] // RANKS
+        for d in range(RANKS):
+            tops = notes[d, from_group] * (scale / (LEVELS * LEVELS))
+            column = jnp.sum(jnp.where(lane == row, tops, 0.0), axis=1, keepdims=True)
+            factor[s, 32 * d:32 * d + 32] = jnp.broadcast_to(column, (32, 128))
+
     def compute(s, carry):
         arrive(land.at[s], recvs.at[2 + s])
-        from_group = table[2 * me + s] // RANKS
 
         def decode(d, inner):
-            rows = pl.ds(pl.multiple_of(32 * d, 32), 32)
-            tops = notes[from_group * RANKS + d] * scale
-            factor = jnp.sum(jnp.where(lane == row, tops, 0.0), axis=1, keepdims=True)
-            code = land[s, rows, :].astype(i32).astype(f32) * (1.0 / LEVELS)
-            high, low = split(code * jnp.abs(code) * factor)
-            grad_s[s, 0, rows, :] = high
-            grad_s[s, 1, rows, :] = low
+            rows = pl.ds(pl.multiple_of(64 * d, 64), 64)
+            for j in range(4):
+                cols = pl.ds(128 * j, 128)
+                code = land[s, rows, cols].astype(i32).astype(f32)
+                grad_s[s, 0, rows, cols], grad_s[s, 1, rows, cols] = split(code * jnp.abs(code) * factor[s, rows])
             return inner
 
-        lax.fori_loop(0, RANKS, decode, 0)
+        lax.fori_loop(0, ORDER // 64, decode, 0)
         lh, ll, rh, rl = basis_s[0, s, 0], basis_s[0, s, 1], basis_s[1, s, 0], basis_s[1, s, 1]
         half_turned = product((lh, ll), (grad_s[s, 0], grad_s[s, 1]), ((0,), (0,)))
         work_s[0], work_s[1] = split(half_turned)
         turned = product((work_s[0], work_s[1]), (rh, rl), ((1,), (0,)))
-        kept = table[2 * N + 2 * me + s] > 0
+        kept = table[2 + s, me] > 0
         moved = jnp.where(kept, 0.9, 1.0) * old_v[0, s] + jnp.where(kept, 0.1, 0.0) * turned
         spread = jnp.where(kept, 0.95, 1.0) * old_v[1, s] + jnp.where(kept, 0.05, 0.0) * turned * turned
         new_first[s] = moved
@@ -172,7 +200,7 @@
     lax.fori_loop(0, 2, compute, 0)
 
     def factors(s, carry):
-        kept = table[2 * N + 2 * me + s] > 0
+        kept = table[2 + s, me] > 0
         stay, fresh = jnp.where(kept, 0.95, 1.0), jnp.where(kept, 0.05, 0.0)
         halves = (grad_s[s, 0], grad_s[s, 1])
         new_left[s] = stay * old_v[2, s] + fresh * product(halves, halves, ((1,), (1,)))
@@ -185,7 +213,7 @@
 
     def collect(g):
         for c in range(RANKS):
-            slot = table[4 * N + RANKS * g + c]
+            slot = table[4, RANKS * g + c]
             send4[g, c] = recv3[slot % 2, slot // 2]
 
     for d in range(1, GROUPS):
@@ -206,40 +234,43 @@
     lax.fori_loop(0, RANKS, unpack, 0)
     others = pl.ds(0, N - 1)
     arrive(send1.at[pl.ds(0, GROUPS - 1)], sends.at[0])
-    arrive(notes.at[others], sends.at[1])
+    arrive(notes1.at[pl.ds(0, GROUPS - 1)], sends.at[1])
+    arrive(notes.at[pl.ds(0, RANKS - 1)], sends.at[5])
     arrive(send4.at[pl.ds(0, GROUPS - 1)], sends.at[4])
     for s in range(2):
         arrive(send2.at[s, others], sends.at[2])
         arrive(recv3.at[s, others], sends.at[3])
 
 
-def block_slots(block_owner):
-    positions = jnp.arange(block_owner.shape[0], dtype=i32)
-    same_owner = block_owner[:, None] == block_owner[None, :]
-    earlier = positions[None, :] < positions[:, None]
-    return jnp.sum(jnp.where(same_owner & earlier, 1, 0), axis=1).astype(i32)
+def settle_kernel(*refs):
+    count = len(refs) // 2
+    copies = [pltpu.make_async_copy(refs[k], refs[count + k], refs[-1].at[k]) for k in range(count)]
+    for copy in copies:
+        copy.start()
+    for copy in copies:
+        copy.wait()
 
 
 def per_device(grad, block_owner, left_factor, right_factor, left_basis, right_basis, first_moment, second_moment):
-    place = 2 * block_owner + block_slots(block_owner)
-    hits = place[None, :] == jnp.arange(2 * N, dtype=i32)[:, None]
-    index = jnp.sum(jnp.where(hits, jnp.arange(N, dtype=i32)[None, :], 0), axis=1)
-    table = jnp.concatenate([index, jnp.any(hits, axis=1).astype(i32), place])
     state = pltpu.VMEM((2, ORDER, ORDER), f32)
     in_hbm = pl.BlockSpec(memory_space=pl.ANY)
     in_vmem = pl.BlockSpec(memory_space=pltpu.VMEM)
-    return pl.pallas_call(
+    results = pl.pallas_call(
         step_kernel,
         out_shape=[pltpu.VMEM(grad.shape, bf16)] + [state] * 4,
-        in_specs=[pl.BlockSpec(memory_space=pltpu.SMEM)] + [in_hbm] * 7,
+        in_specs=[in_vmem] + [in_hbm] * 7,
         out_specs=[in_vmem] * 5,
         scratch_shapes=[
+            pltpu.VMEM((8, N), i32),
+            pltpu.SMEM((8, N), i32),
+            pltpu.VMEM((2, ORDER, 128), f32),
             pltpu.VMEM(grad.shape, f32),
             pltpu.VMEM((2, 2, ORDER, ORDER), f32),
             pltpu.VMEM((4, 2, ORDER, ORDER), f32),
             pltpu.VMEM((2, 2, 2, ORDER, ORDER), bf16),
             pltpu.VMEM((1, 128), f32),
-            pltpu.VMEM((N, 1, 128), f32),
+            pltpu.VMEM((GROUPS, 1, 128), f32),
+            pltpu.VMEM((RANKS, GROUPS, 1, 128), f32),
             pltpu.VMEM((GROUPS, RANKS, 16, 128), i16),
             pltpu.VMEM((GROUPS, RANKS, 16, 128), i16),
             pltpu.VMEM((2, N, 16, 128), i16),
@@ -250,14 +281,23 @@
             pltpu.VMEM((2, N, 16, 128), bf16),
             pltpu.VMEM((GROUPS, RANKS, 16, 128), bf16),
             pltpu.VMEM((GROUPS, RANKS, 16, 128), bf16),
+            pltpu.SemaphoreType.DMA((8,)),
+            pltpu.SemaphoreType.DMA((6,)),
             pltpu.SemaphoreType.DMA((7,)),
-            pltpu.SemaphoreType.DMA((5,)),
-            pltpu.SemaphoreType.DMA((6,)),
         ],
         compiler_params=pltpu.CompilerParams(
             collective_id=0, has_side_effects=True, vmem_limit_bytes=50 * 2**20),
         name="soap_step",
-    )(table, grad, left_basis, right_basis, first_moment, second_moment, left_factor, right_factor)
+    )(block_owner.reshape(1, N), grad, left_basis, right_basis, first_moment, second_moment, left_factor, right_factor)
+    return pl.pallas_call(
+        settle_kernel,
+        out_shape=[jax.ShapeDtypeStruct(r.shape, r.dtype) for r in results],
+        in_specs=[in_hbm] * 5,
+        out_specs=[in_hbm] * 5,
+        scratch_shapes=[pltpu.SemaphoreType.DMA((5,))],
+        compiler_params=pltpu.CompilerParams(vmem_limit_bytes=2**20),
+        name="settle",
+    )(*results)
 
 
 def solution(mesh):

time: 73.9 us -> 67.7 us (0.916)
  local copies, waits for them, and re-layouts: 6.07 us -> 0 us
  other arithmetic: 2.41 us -> 0 us
  Pallas kernels: 64.6 us -> 67 us
    unnamed x5 -> x0, local copies, waits for them, and re-layouts: 6.07 us -> none
    pallas_call x0 -> x1, Pallas kernels: none -> 3.55 us  [per_device(): pl.pallas_call(settle_kernel, out_shape=[jax.ShapeDtypeStruct(r.shape, r....]
    pallas_call x1, Pallas kernels: 64.6 us -> 63.4 us  [per_device(): pl.pallas_call(step_kernel, out_shape=[pltpu.VMEM(grad.shape, bf16)] + [s...]
    reduce_sum x2 -> x0, other arithmetic: 1.01 us -> none  [the longest x1 0.9 us: block_slots(): return jnp.sum(jnp.where(same_owner & earlier, 1, 0), axis=1).astype(i32)]
where the time goes in v3:
time: 67.7 us; the launch traced here: 67.6 us
  Pallas kernels  67 us (99%)
    pallas_call x1, Pallas kernels, per_device(): pl.pallas_call(step_kernel, out_shape=[pltpu.VMEM(grad.shape, bf16)] + [s...  63.4 us
    pallas_call x1, Pallas kernels, per_device(): pl.pallas_call(settle_kernel, out_shape=[jax.ShapeDtypeStruct(r.shape, r....  3.55 us

profile of v3, /device:TPU:0, one launch (start us, length us, event | category | flops | bytes accessed | tf_op | source)
XLA Modules:
  0.0 67.6 jit_solution(12187214668182781379)
XLA Ops:
  0.6 63.4 %soap_step.1 = (bf16[32,8192]{1,0:T(8,128)(2,1)S(1)}, f32[2,512,512]{2,1,0:T(8,128)S(1)}, f32[2,512,512]{2,1,0:T(8,128)S(1)}, f32[2,512,512]{2,1,0:T(8,128)S(1)}, f32[2,512,512]{2,1,0:T(8,128)S(1)}) custom-call(s32[1,128]{1,0:T(1,128)} %bitcast.1, f32[32,8192]{1,0:T(8,128)} %grad.1, f32[2,512,512]{2,1,0:T(8,128)} %left_basis.1, f32[2,512,512]{2,1,0:T(8,128)} %right_basis.1, ...), custom_call_target="tpu_custom_call" | custom-call | tf_op jit(solution)/shard_map/soap_step/pallas_call | solution.py:258
  64.1 3.5 %settle.1 = (bf16[32,8192]{1,0:T(8,128)(2,1)}, f32[2,512,512]{2,1,0:T(8,128)}, f32[2,512,512]{2,1,0:T(8,128)}, f32[2,512,512]{2,1,0:T(8,128)}, f32[2,512,512]{2,1,0:T(8,128)}) custom-call(bf16[32,8192]{1,0:T(8,128)(2,1)S(1)} %get-tuple-element.10.refs_0_, f32[2,512,512]{2,1,0:T(8,128)S(1)} %get-tuple-element.11.refs_1_, ...), custom_call_target="tpu_custom_call" | custom-call | tf_op jit(solution)/shard_map/settle/pallas_call | solution.py:292

commit v4 on v3

--- a/solution.py
+++ b/solution.py
@@ -53,7 +53,7 @@
     owner, grad, left_basis, right_basis, first, second, left, right,
     updates, new_left, new_right, new_first, new_second,
     table_v, table, factor, grad_v, basis_v, old_v, basis_s, note, notes1, notes, send1, recv1, send2, land, grad_s, work_s, back, recv3, send4, recv4,
-    loads, sends, recvs,
+    loads, sends, recvs, arrivals, groups_in,
 ):
     me = lax.axis_index("dp")
     group, rank = me // RANKS, me % RANKS
@@ -62,27 +62,31 @@
     pairs = [(grad, grad_v), (left_basis, basis_v.at[0]), (right_basis, basis_v.at[1]), (first, old_v.at[0]),
              (second, old_v.at[1]), (left, old_v.at[2]), (right, old_v.at[3])]
     copies = [pltpu.make_async_copy(src, dst, loads.at[k]) for k, (src, dst) in enumerate(pairs)]
-    for copy in copies:
-        copy.start()
+    copies[0].start()
     barrier = pltpu.get_barrier_semaphore()
-    each_peer(me, lambda peer: pl.semaphore_signal(barrier, inc=1, device_id=(peer,), device_id_type=MESH))
+    same_rank = [lax.rem(group + d, GROUPS) * RANKS + rank for d in range(1, GROUPS)]
+    same_group = [group * RANKS + lax.rem(rank + d, RANKS) for d in range(1, RANKS)]
+    for peer in same_rank + same_group:
+        pl.semaphore_signal(barrier, inc=1, device_id=(peer,), device_id_type=MESH)
 
     above = lax.broadcasted_iota(i32, (N, N), 0)
     along = lax.broadcasted_iota(i32, (N, N), 1)
     owners = jnp.broadcast_to(owner[...], (N, N))
     earlier = jnp.where((owners == owners.T) & (above < along), 1, 0)
-    places = 2 * owner[...] + jnp.sum(earlier, axis=0, keepdims=True)
+    places = owner[...] + N * jnp.sum(earlier, axis=0, keepdims=True)
     turned_places = jnp.broadcast_to(places, (N, N)).T
     for s in range(2):
-        hits = turned_places == 2 * along + s
+        hits = turned_places == along + N * s
         table_v[s:s + 1] = jnp.sum(jnp.where(hits, above, 0), axis=0, keepdims=True)
         table_v[2 + s:3 + s] = jnp.sum(jnp.where(hits, 1, 0), axis=0, keepdims=True)
-    table_v[4:5] = places
+    table_v[4:5] = jnp.minimum(places, 2 * N - 1)
     table_v[5:8] = jnp.zeros((3, N), i32)
     table_copy = pltpu.make_async_copy(table_v, table, loads.at[7])
     table_copy.start()
 
     copies[0].wait()
+    for copy in copies[1:]:
+        copy.start()
     values = grad_v[...]
     top = jnp.max(jnp.abs(values), axis=1, keepdims=True)
     squares = jnp.sum(values * values)
@@ -102,20 +106,24 @@
         return carry
 
     lax.fori_loop(0, RANKS, encode, 0)
-    pl.semaphore_wait(barrier, N - 1)
-
+    pl.semaphore_wait(barrier, len(same_rank) + len(same_group))
+    for peer in same_rank:
+        pl.semaphore_signal(groups_in, inc=1, device_id=(peer,), device_id_type=MESH)
+
+    own_blocks = pl.ds(group * RANKS, RANKS)
     for d in range(1, GROUPS):
         to = lax.rem(group + d, GROUPS)
         remote(note, notes1.at[group], sends.at[1], recvs.at[1], to * RANKS + rank)
-        remote(send1.at[to], recv1.at[group], sends.at[0], recvs.at[0], to * RANKS + rank)
+        remote(send1.at[to], recv1.at[own_blocks], sends.at[0], recvs.at[0], to * RANKS + rank)
     pltpu.make_async_copy(note, notes1.at[group], recvs.at[1]).start()
-    pltpu.make_async_copy(send1.at[group], recv1.at[group], recvs.at[0]).start()
+    pltpu.make_async_copy(send1.at[group], recv1.at[own_blocks], recvs.at[0]).start()
 
     for k in range(2):
         copies[1 + k].wait()
         for s in range(2):
             basis_s[k, s, 0], basis_s[k, s, 1] = split(basis_v[k, s])
     table_copy.wait()
+    pl.semaphore_wait(groups_in, len(same_rank))
     arrive(notes1, recvs.at[1])
     arrive(recv1, recvs.at[0])
 
@@ -126,8 +134,7 @@
         place = land.at[s, pl.ds(at_row, 16), pl.ds(at_col, 128)]
 
         def pack(peer):
-            block = table[s, peer]
-            send2[s, peer] = recv1[block // RANKS, block % RANKS]
+            send2[s, peer] = recv1[table[s, peer]]
 
         def post(peer):
             pack(peer)
@@ -186,15 +193,13 @@
         work_s[0], work_s[1] = split(direction)
         half_back = product((lh, ll), (work_s[0], work_s[1]), ((1,), (0,)))
         work_s[0], work_s[1] = split(half_back)
-        back[s] = product((work_s[0], work_s[1]), (rh, rl), ((1,), (1,))).astype(bf16)
-
-        def place(peer):
-            peer_row = pl.multiple_of(32 * (peer % RANKS) + 16 * (peer // 64), 16)
-            peer_col = pl.multiple_of(128 * ((peer // RANKS) % 4), 128)
-            return back.at[s, pl.ds(peer_row, 16), pl.ds(peer_col, 128)]
-
-        each_peer(me, lambda peer: remote(place(peer), recv3.at[s, me], sends.at[3], recvs.at[4], peer))
-        pltpu.make_async_copy(place(me), recv3.at[s, me], recvs.at[4]).start()
+        update = product((work_s[0], work_s[1]), (rh, rl), ((1,), (1,))).astype(bf16)
+        for i in range(N):
+            top_row, left_col = 32 * (i % RANKS) + 16 * (i // 64), 128 * (i // RANKS % 4)
+            back[s, i] = update[top_row:top_row + 16, left_col:left_col + 128]
+        mine = recv3.at[s * N + me]
+        each_peer(me, lambda peer: remote(back.at[s, peer], mine, sends.at[3], recvs.at[4], peer))
+        pltpu.make_async_copy(back.at[s, me], mine, recvs.at[4]).start()
         return carry
 
     lax.fori_loop(0, 2, compute, 0)
@@ -213,25 +218,22 @@
 
     def collect(g):
         for c in range(RANKS):
-            slot = table[4, RANKS * g + c]
-            send4[g, c] = recv3[slot % 2, slot // 2]
+            send4[g, c] = recv3[table[4, RANKS * g + c]]
 
     for d in range(1, GROUPS):
         to = lax.rem(group + d, GROUPS)
         collect(to)
-        remote(send4.at[to], recv4.at[group], sends.at[4], recvs.at[5], to * RANKS + rank)
+        remote(send4.at[to], recv4.at[group], sends.at[4], arrivals.at[d], to * RANKS + rank)
     collect(group)
-    pltpu.make_async_copy(send4.at[group], recv4.at[group], recvs.at[5]).start()
-    arrive(recv4, recvs.at[5])
-
-    def unpack(c, carry):
-        for h in range(2):
-            for j in range(4):
-                col = pl.multiple_of(ORDER * c + 128 * j, 128)
-                updates[16 * h:16 * h + 16, pl.ds(col, 128)] = recv4[4 * h + j, c]
-        return carry
-
-    lax.fori_loop(0, RANKS, unpack, 0)
+    pltpu.make_async_copy(send4.at[group], recv4.at[group], arrivals.at[0]).start()
+    for d in range(GROUPS):
+        source = lax.rem(group + GROUPS - d, GROUPS)
+        arrive(recv4.at[source], arrivals.at[d])
+        source_row = pl.multiple_of(16 * (source // 4), 16)
+        source_col = 128 * lax.rem(source, 4)
+        for c in range(RANKS):
+            col = pl.multiple_of(ORDER * c + source_col, 128)
+            updates[pl.ds(source_row, 16), pl.ds(col, 128)] = recv4[source, c]
     others = pl.ds(0, N - 1)
     arrive(send1.at[pl.ds(0, GROUPS - 1)], sends.at[0])
     arrive(notes1.at[pl.ds(0, GROUPS - 1)], sends.at[1])
@@ -239,7 +241,7 @@
     arrive(send4.at[pl.ds(0, GROUPS - 1)], sends.at[4])
     for s in range(2):
         arrive(send2.at[s, others], sends.at[2])
-        arrive(recv3.at[s, others], sends.at[3])
+        arrive(recv3.at[others], sends.at[3])
 
 
 def settle_kernel(*refs):
@@ -272,18 +274,20 @@
             pltpu.VMEM((GROUPS, 1, 128), f32),
             pltpu.VMEM((RANKS, GROUPS, 1, 128), f32),
             pltpu.VMEM((GROUPS, RANKS, 16, 128), i16),
-            pltpu.VMEM((GROUPS, RANKS, 16, 128), i16),
+            pltpu.VMEM((N, 16, 128), i16),
             pltpu.VMEM((2, N, 16, 128), i16),
             pltpu.VMEM((2, ORDER, ORDER), i16),
             pltpu.VMEM((2, 2, ORDER, ORDER), bf16),
             pltpu.VMEM((2, ORDER, ORDER), bf16),
-            pltpu.VMEM((2, ORDER, ORDER), bf16),
             pltpu.VMEM((2, N, 16, 128), bf16),
+            pltpu.VMEM((2 * N, 16, 128), bf16),
             pltpu.VMEM((GROUPS, RANKS, 16, 128), bf16),
             pltpu.VMEM((GROUPS, RANKS, 16, 128), bf16),
             pltpu.SemaphoreType.DMA((8,)),
             pltpu.SemaphoreType.DMA((6,)),
             pltpu.SemaphoreType.DMA((7,)),
+            pltpu.SemaphoreType.DMA((GROUPS,)),
+            pltpu.SemaphoreType.REGULAR,
         ],
         compiler_params=pltpu.CompilerParams(
             collective_id=0, has_side_effects=True, vmem_limit_bytes=50 * 2**20),

time: 67.7 us -> 64.6 us (0.954); the launches traced: 67.6 us -> 63.4 us
  Pallas kernels: 67 us -> 62.8 us
    pallas_call x1, Pallas kernels: 63.4 us -> 59.2 us  [per_device(): pl.pallas_call(step_kernel, out_shape=[pltpu.VMEM(grad.shape, bf16)] + [s...]
where the time goes in v4:
time: 64.6 us; the launch traced here: 63.4 us
  Pallas kernels  62.8 us (97%)
    pallas_call x1, Pallas kernels, per_device(): pl.pallas_call(step_kernel, out_shape=[pltpu.VMEM(grad.shape, bf16)] + [s...  59.2 us
    pallas_call x1, Pallas kernels, per_device(): pl.pallas_call(settle_kernel, out_shape=[jax.ShapeDtypeStruct(r.shape, r....  3.55 us

profile of v4, /device:TPU:0, one launch (start us, length us, event | category | flops | bytes accessed | tf_op | source)
XLA Modules:
  0.0 63.4 jit_solution(15720774432670981049)
XLA Ops:
  0.6 59.2 %soap_step.1 = (bf16[32,8192]{1,0:T(8,128)(2,1)S(1)}, f32[2,512,512]{2,1,0:T(8,128)S(1)}, f32[2,512,512]{2,1,0:T(8,128)S(1)}, f32[2,512,512]{2,1,0:T(8,128)S(1)}, f32[2,512,512]{2,1,0:T(8,128)S(1)}) custom-call(s32[1,128]{1,0:T(1,128)} %bitcast.1, f32[32,8192]{1,0:T(8,128)} %grad.1, f32[2,512,512]{2,1,0:T(8,128)} %left_basis.1, f32[2,512,512]{2,1,0:T(8,128)} %right_basis.1, ...), custom_call_target="tpu_custom_call" | custom-call | tf_op jit(solution)/shard_map/soap_step/pallas_call | solution.py:260
  59.8 3.5 %settle.1 = (bf16[32,8192]{1,0:T(8,128)(2,1)}, f32[2,512,512]{2,1,0:T(8,128)}, f32[2,512,512]{2,1,0:T(8,128)}, f32[2,512,512]{2,1,0:T(8,128)}, f32[2,512,512]{2,1,0:T(8,128)}) custom-call(bf16[32,8192]{1,0:T(8,128)(2,1)S(1)} %get-tuple-element.10.refs_0_, f32[2,512,512]{2,1,0:T(8,128)S(1)} %get-tuple-element.11.refs_1_, ...), custom_call_target="tpu_custom_call" | custom-call | tf_op jit(solution)/shard_map/settle/pallas_call | solution.py:296

commit v5 on v4

--- a/solution.py
+++ b/solution.py
@@ -11,7 +11,7 @@
 RANKS = 16
 ORDER = 512
 STRIDE = 45
-UNROLL = 8
+UNROLL = 16
 LEVELS = 32767.0
 FIRST_CORRECTION = 1.0 - 0.9**10
 SECOND_CORRECTION = 1.0 - 0.95**10
@@ -52,7 +52,7 @@
 def step_kernel(
     owner, grad, left_basis, right_basis, first, second, left, right,
     updates, new_left, new_right, new_first, new_second,
-    table_v, table, factor, grad_v, basis_v, old_v, basis_s, note, notes1, notes, send1, recv1, send2, land, grad_s, work_s, back, recv3, send4, recv4,
+    table_v, table, factor, grad_v, basis_v, old_v, basis_s, note, notes1, notes, inverse_v, send1, recv1, send2, land, grad_s, work_s, back, recv3, send4, recv4,
     loads, sends, recvs, arrivals, groups_in,
 ):
     me = lax.axis_index("dp")
@@ -68,6 +68,44 @@
     same_group = [group * RANKS + lax.rem(rank + d, RANKS) for d in range(1, RANKS)]
     for peer in same_rank + same_group:
         pl.semaphore_signal(barrier, inc=1, device_id=(peer,), device_id_type=MESH)
+
+    copies[0].wait()
+    values = grad_v[...]
+    top = jnp.max(jnp.abs(values), axis=1, keepdims=True)
+    squares = jnp.sum(values * values)
+    inverse = jnp.where(top > 1e-37, 1.0 / jnp.maximum(top, 1e-37), 0.0)
+    row = lax.broadcasted_iota(i32, (32, 128), 0)
+    lane = lax.broadcasted_iota(i32, (32, 128), 1)
+    tops = jnp.sum(jnp.where(lane == row, top, 0.0), axis=0, keepdims=True)
+    note[...] = tops + jnp.where(lane[:1] == 32, squares, 0.0)
+
+    def encode(to):
+        rows = pl.ds(pl.multiple_of(16 * (to // 4), 16), 16)
+        scales = inverse_v[rows]
+        for c in range(RANKS):
+            tile = grad_v[rows, pl.ds(pl.multiple_of(ORDER * c + 128 * (to % 4), 128), 128)]
+            code = (jnp.sqrt(jnp.abs(tile) * scales) * LEVELS + 0.5).astype(i32)
+            send1[to, c] = jnp.where(tile < 0.0, -code, code).astype(i16)
+
+    inverse_v[...] = jnp.broadcast_to(inverse, (32, 128))
+    own_blocks = pl.ds(group * RANKS, RANKS)
+    pl.semaphore_wait(barrier, len(same_rank) + len(same_group))
+
+    def spread(d, carry):
+        to = lax.rem(group + d, GROUPS)
+        peer = to * RANKS + rank
+        encode(to)
+        remote(send1.at[to], recv1.at[own_blocks], sends.at[0], recvs.at[0], peer)
+        remote(note, notes1.at[group], sends.at[1], recvs.at[1], peer)
+        pl.semaphore_signal(groups_in, inc=1, device_id=(peer,), device_id_type=MESH)
+        return carry
+
+    lax.fori_loop(1, GROUPS, spread, 0)
+    for copy in copies[1:]:
+        copy.start()
+    encode(group)
+    pltpu.make_async_copy(send1.at[group], recv1.at[own_blocks], recvs.at[0]).start()
+    pltpu.make_async_copy(note, notes1.at[group], recvs.at[1]).start()
 
     above = lax.broadcasted_iota(i32, (N, N), 0)
     along = lax.broadcasted_iota(i32, (N, N), 1)
@@ -84,40 +122,6 @@
     table_copy = pltpu.make_async_copy(table_v, table, loads.at[7])
     table_copy.start()
 
-    copies[0].wait()
-    for copy in copies[1:]:
-        copy.start()
-    values = grad_v[...]
-    top = jnp.max(jnp.abs(values), axis=1, keepdims=True)
-    squares = jnp.sum(values * values)
-    inverse = jnp.where(top > 1e-37, 1.0 / jnp.maximum(top, 1e-37), 0.0)
-    row = lax.broadcasted_iota(i32, (32, 128), 0)
-    lane = lax.broadcasted_iota(i32, (32, 128), 1)
-    tops = jnp.sum(jnp.where(lane == row, top, 0.0), axis=0, keepdims=True)
-    note[...] = tops + jnp.where(lane[:1] == 32, squares, 0.0)
-
-    def encode(c, carry):
-        for h in range(2):
-            for j in range(4):
-                col = pl.multiple_of(ORDER * c + 128 * j, 128)
-                tile = grad_v[16 * h:16 * h + 16, pl.ds(col, 128)]
-                code = (jnp.sqrt(jnp.abs(tile) * inverse[16 * h:16 * h + 16]) * LEVELS + 0.5).astype(i32)
-                send1[4 * h + j, c] = jnp.where(tile < 0.0, -code, code).astype(i16)
-        return carry
-
-    lax.fori_loop(0, RANKS, encode, 0)
-    pl.semaphore_wait(barrier, len(same_rank) + len(same_group))
-    for peer in same_rank:
-        pl.semaphore_signal(groups_in, inc=1, device_id=(peer,), device_id_type=MESH)
-
-    own_blocks = pl.ds(group * RANKS, RANKS)
-    for d in range(1, GROUPS):
-        to = lax.rem(group + d, GROUPS)
-        remote(note, notes1.at[group], sends.at[1], recvs.at[1], to * RANKS + rank)
-        remote(send1.at[to], recv1.at[own_blocks], sends.at[0], recvs.at[0], to * RANKS + rank)
-    pltpu.make_async_copy(note, notes1.at[group], recvs.at[1]).start()
-    pltpu.make_async_copy(send1.at[group], recv1.at[own_blocks], recvs.at[0]).start()
-
     for k in range(2):
         copies[1 + k].wait()
         for s in range(2):
@@ -189,7 +193,7 @@
         spread = jnp.where(kept, 0.95, 1.0) * old_v[1, s] + jnp.where(kept, 0.05, 0.0) * turned * turned
         new_first[s] = moved
         new_second[s] = spread
-        direction = moved / FIRST_CORRECTION / (jnp.sqrt(spread / SECOND_CORRECTION) + 1e-08)
+        direction = moved * (1.0 / FIRST_CORRECTION) / (jnp.sqrt(spread * (1.0 / SECOND_CORRECTION)) + 1e-08)
         work_s[0], work_s[1] = split(direction)
         half_back = product((lh, ll), (work_s[0], work_s[1]), ((1,), (0,)))
         work_s[0], work_s[1] = split(half_back)
@@ -273,6 +277,7 @@
             pltpu.VMEM((1, 128), f32),
             pltpu.VMEM((GROUPS, 1, 128), f32),
             pltpu.VMEM((RANKS, GROUPS, 1, 128), f32),
+            pltpu.VMEM((32, 128), f32),
             pltpu.VMEM((GROUPS, RANKS, 16, 128), i16),
             pltpu.VMEM((N, 16, 128), i16),
             pltpu.VMEM((2, N, 16, 128), i16),

time: 64.6 us -> 63.6 us (0.985); the launches traced: 63.4 us -> 63.4 us
  no operation moved by 1% of the time
where the time goes in v5:
time: 63.6 us; the launch traced here: 63.4 us
  Pallas kernels  62.8 us (99%)
  between operations  0.64 us (1%)
    pallas_call x1, Pallas kernels, per_device(): pl.pallas_call(step_kernel, out_shape=[pltpu.VMEM(grad.shape, bf16)] + [s...  59.2 us
    pallas_call x1, Pallas kernels, per_device(): pl.pallas_call(settle_kernel, out_shape=[jax.ShapeDtypeStruct(r.shape, r....  3.55 us

profile of v5, /device:TPU:0, one launch (start us, length us, event | category | flops | bytes accessed | tf_op | source)
XLA Modules:
  0.0 63.4 jit_solution(6863104404594733255)
XLA Ops:
  0.6 59.2 %soap_step.1 = (bf16[32,8192]{1,0:T(8,128)(2,1)S(1)}, f32[2,512,512]{2,1,0:T(8,128)S(1)}, f32[2,512,512]{2,1,0:T(8,128)S(1)}, f32[2,512,512]{2,1,0:T(8,128)S(1)}, f32[2,512,512]{2,1,0:T(8,128)S(1)}) custom-call(s32[1,128]{1,0:T(1,128)} %bitcast.1, f32[32,8192]{1,0:T(8,128)} %grad.1, f32[2,512,512]{2,1,0:T(8,128)} %left_basis.1, f32[2,512,512]{2,1,0:T(8,128)} %right_basis.1, ...), custom_call_target="tpu_custom_call" | custom-call | tf_op jit(solution)/shard_map/soap_step/pallas_call | solution.py:264
  59.9 3.5 %settle.1 = (bf16[32,8192]{1,0:T(8,128)(2,1)}, f32[2,512,512]{2,1,0:T(8,128)}, f32[2,512,512]{2,1,0:T(8,128)}, f32[2,512,512]{2,1,0:T(8,128)}, f32[2,512,512]{2,1,0:T(8,128)}) custom-call(bf16[32,8192]{1,0:T(8,128)(2,1)S(1)} %get-tuple-element.10.refs_0_, f32[2,512,512]{2,1,0:T(8,128)S(1)} %get-tuple-element.11.refs_1_, ...), custom_call_target="tpu_custom_call" | custom-call | tf_op jit(solution)/shard_map/settle/pallas_call | solution.py:301

commit v6 on v5

--- a/solution.py
+++ b/solution.py
@@ -52,7 +52,7 @@
 def step_kernel(
     owner, grad, left_basis, right_basis, first, second, left, right,
     updates, new_left, new_right, new_first, new_second,
-    table_v, table, factor, grad_v, basis_v, old_v, basis_s, note, notes1, notes, inverse_v, send1, recv1, send2, land, grad_s, work_s, back, recv3, send4, recv4,
+    table_v, table, factor, grad_v, basis_v, old_v, basis_s, turned_s, note, notes1, notes, inverse_v, send1, recv1, send2, land, grad_s, work_s, back, recv3, send4, recv4,
     loads, sends, recvs, arrivals, groups_in,
 ):
     me = lax.axis_index("dp")
@@ -126,6 +126,7 @@
         copies[1 + k].wait()
         for s in range(2):
             basis_s[k, s, 0], basis_s[k, s, 1] = split(basis_v[k, s])
+            turned_s[k, s, 0], turned_s[k, s, 1] = split(basis_v[k, s].T)
     table_copy.wait()
     pl.semaphore_wait(groups_in, len(same_rank))
     arrive(notes1, recvs.at[1])
@@ -185,7 +186,7 @@
 
         lax.fori_loop(0, ORDER // 64, decode, 0)
         lh, ll, rh, rl = basis_s[0, s, 0], basis_s[0, s, 1], basis_s[1, s, 0], basis_s[1, s, 1]
-        half_turned = product((lh, ll), (grad_s[s, 0], grad_s[s, 1]), ((0,), (0,)))
+        half_turned = product((turned_s[0, s, 0], turned_s[0, s, 1]), (grad_s[s, 0], grad_s[s, 1]), ((1,), (0,)))
         work_s[0], work_s[1] = split(half_turned)
         turned = product((work_s[0], work_s[1]), (rh, rl), ((1,), (0,)))
         kept = table[2 + s, me] > 0
@@ -197,7 +198,7 @@
         work_s[0], work_s[1] = split(direction)
         half_back = product((lh, ll), (work_s[0], work_s[1]), ((1,), (0,)))
         work_s[0], work_s[1] = split(half_back)
-        update = product((work_s[0], work_s[1]), (rh, rl), ((1,), (1,))).astype(bf16)
+        update = product((work_s[0], work_s[1]), (turned_s[1, s, 0], turned_s[1, s, 1]), ((1,), (0,))).astype(bf16)
         for i in range(N):
             top_row, left_col = 32 * (i % RANKS) + 16 * (i // 64), 128 * (i // RANKS % 4)
             back[s, i] = update[top_row:top_row + 16, left_col:left_col + 128]
@@ -273,6 +274,7 @@
             pltpu.VMEM(grad.shape, f32),
             pltpu.VMEM((2, 2, ORDER, ORDER), f32),
             pltpu.VMEM((4, 2, ORDER, ORDER), f32),
+            pltpu.VMEM((2, 2, 2, ORDER, ORDER), bf16),
             pltpu.VMEM((2, 2, 2, ORDER, ORDER), bf16),
             pltpu.VMEM((1, 128), f32),
             pltpu.VMEM((GROUPS, 1, 128), f32),

time: 63.6 us -> 63.5 us (level)
  no operation moved by 1% of the time
where the time goes in v6:
time: 63.5 us; the launch traced here: 63.4 us
  Pallas kernels  62.7 us (99%)
  between operations  0.64 us (1%)
    pallas_call x1, Pallas kernels, per_device(): pl.pallas_call(step_kernel, out_shape=[pltpu.VMEM(grad.shape, bf16)] + [s...  59.2 us
    pallas_call x1, Pallas kernels, per_device(): pl.pallas_call(settle_kernel, out_shape=[jax.ShapeDtypeStruct(r.shape, r....  3.55 us

profile of v6, /device:TPU:0, one launch (start us, length us, event | category | flops | bytes accessed | tf_op | source)
XLA Modules:
  0.0 63.4 jit_solution(1312053765577923742)
XLA Ops:
  0.6 59.2 %soap_step.1 = (bf16[32,8192]{1,0:T(8,128)(2,1)S(1)}, f32[2,512,512]{2,1,0:T(8,128)S(1)}, f32[2,512,512]{2,1,0:T(8,128)S(1)}, f32[2,512,512]{2,1,0:T(8,128)S(1)}, f32[2,512,512]{2,1,0:T(8,128)S(1)}) custom-call(s32[1,128]{1,0:T(1,128)} %bitcast.1, f32[32,8192]{1,0:T(8,128)} %grad.1, f32[2,512,512]{2,1,0:T(8,128)} %left_basis.1, f32[2,512,512]{2,1,0:T(8,128)} %right_basis.1, ...), custom_call_target="tpu_custom_call" | custom-call | tf_op jit(solution)/shard_map/soap_step/pallas_call | solution.py:265
  59.8 3.5 %settle.1 = (bf16[32,8192]{1,0:T(8,128)(2,1)}, f32[2,512,512]{2,1,0:T(8,128)}, f32[2,512,512]{2,1,0:T(8,128)}, f32[2,512,512]{2,1,0:T(8,128)}, f32[2,512,512]{2,1,0:T(8,128)}) custom-call(bf16[32,8192]{1,0:T(8,128)(2,1)S(1)} %get-tuple-element.10.refs_0_, f32[2,512,512]{2,1,0:T(8,128)S(1)} %get-tuple-element.11.refs_1_, ...), custom_call_target="tpu_custom_call" | custom-call | tf_op jit(solution)/shard_map/settle/pallas_call | solution.py:303
